TPU v7x, 32 devices: a whole 2x2x4 slice. The times are simulated.
32 devices in a mesh: scalar: 4 (over z), space: 8 (over y, x, core).
Axes of the slice: x: 2, y: 2, z: 4, core: 2. Of those that a mesh axis runs over, the one named last changes fastest.
Arguments:
- scalars: float32 [16, 2, 1024, 1024], P('scalar', None, 'space'), may hold values from -6 to 6
- velocity_x: float32 [2, 1024, 1024], P(None, 'space', 'scalar'), may hold values from 0 to 1, as said below
- velocity_y: float32 [2, 1024, 1024], P(None, 'space', 'scalar'), may hold values from 0 to 1, as said below
- shift_x: int32 [2, 1024], P(None, 'space'), may hold values from -8 to 8
- shift_y: int32 [1024], P('space'), may hold values from -8 to 8
- schmidt: int32 [16], P('scalar'), may hold values from 1 to 5
Outputs:
- transported: float32 [16, 2, 1024, 1024], P('scalar', None, 'space')
Inputs may be any that keep to these rules, and one draw needn't show every extreme that they name: shift_x and shift_y are whole cells of displacement along the line; they act periodically. `velocity_x`: fractions of a cell. `velocity_y`: fractions of a cell.
All inputs are finite; a program needn't handle non-finite values.
Results may differ from a plain program's by a relative error of at most 0.0003.
Values sent between devices are 32-bit elements; how exact they have to be, the bound alone decides.
A program may use at most 192 MiB of HBM per device.

v0:
```python
import math

import jax
import jax.numpy as jnp
from jax import lax
from jax.sharding import PartitionSpec as P

NY = 1024


def spline(distance):
    magnitude = jnp.abs(distance)
    far_part = jnp.maximum(3.0 - magnitude, 0.0)
    middle = jnp.maximum(2.0 - magnitude, 0.0)
    near_part = jnp.maximum(1.0 - magnitude, 0.0)
    return (far_part**5 - 6.0 * middle**5 + 15.0 * near_part**5) / 120.0


def remesh(fields, fraction, shift_line):
    summed = jnp.zeros_like(fields)
    for offset in range(-2, 4):
        weight = spline(offset - fraction)
        summed = summed + jnp.roll(fields * weight, offset, axis=-1)
    line_shift = shift_line[None, :, :, None]
    moved = summed
    for amount in range(-8, 9):
        moved = jnp.where(line_shift == amount, jnp.roll(summed, amount, axis=-1), moved)
    return moved


def remesh_columns(fields, fraction, shift_cols):
    summed = jnp.zeros_like(fields)
    for offset in range(-2, 4):
        weight = spline(offset - fraction)
        summed = summed + jnp.roll(fields * weight[None], offset, axis=2)
    column_shift = shift_cols[None, None, None, :]
    moved = summed
    for amount in range(-8, 9):
        moved = jnp.where(column_shift == amount, jnp.roll(summed, amount, axis=2), moved)
    return moved


def spectral_tables(length):
    midpoint = length // 2
    column = jnp.arange(length, dtype=jnp.int32)
    wavenum = jnp.where(column <= midpoint, column, column - midpoint)
    phases = column[:, None] * wavenum[None, :] % length
    angles = phases.astype(jnp.float32) * (2.0 * math.pi / length)
    forward = jnp.where((column <= midpoint)[None, :], jnp.cos(angles), jnp.sin(angles))
    inverse_weight = jnp.where((wavenum == 0) | (column == midpoint), 1.0, 2.0) / length
    inverse = forward.T * inverse_weight[:, None]
    relative = wavenum.astype(jnp.float32) / midpoint
    return (forward, inverse, relative * relative)


def diffuse(fields, diffusivity, tables):
    forward, inverse, wave_square = tables
    initial = fields.shape
    rows_flat = fields.reshape(-1, initial[-1])
    spectra = jnp.dot(
        rows_flat, forward, precision=lax.Precision.HIGHEST, preferred_element_type=jnp.float32
    )
    damping = jnp.exp(-diffusivity[:, None] * wave_square[None, :])
    spectra = spectra.reshape(initial) * damping[:, None, None, :]
    result = jnp.dot(
        spectra.reshape(-1, initial[-1]),
        inverse,
        precision=lax.Precision.HIGHEST,
        preferred_element_type=jnp.float32,
    )
    return result.reshape(initial)


def diffuse_columns(fields, diffusivity, tables):
    forward, inverse, wave_square = tables
    spectra = jnp.einsum(
        "jk,szjx->szkx",
        forward,
        fields,
        precision=lax.Precision.HIGHEST,
        preferred_element_type=jnp.float32,
    )
    damping = jnp.exp(-diffusivity[:, None] * wave_square[None, :])
    spectra = spectra * damping[:, None, :, None]
    return jnp.einsum(
        "kj,szkx->szjx",
        inverse,
        spectra,
        precision=lax.Precision.HIGHEST,
        preferred_element_type=jnp.float32,
    )


def one_sweep(fields, fraction, shift_line, diffusivity, tables):
    return diffuse(remesh(fields, fraction, shift_line), diffusivity, tables)


def fetch_velocity(velocity_x):
    return lax.all_gather(velocity_x, "scalar", axis=2, tiled=True)


def on_device(scalars, velocity_x, velocity_y, shift_x, shift_y, schmidt):
    diffusivity = jnp.exp2((3 - schmidt).astype(jnp.float32))
    tables_x = spectral_tables(scalars.shape[3])
    tables_y = spectral_tables(NY)
    along_x = fetch_velocity(velocity_x)
    fields = one_sweep(scalars, along_x, shift_x, 0.5 * diffusivity, tables_x)
    along_y = lax.all_gather(velocity_y, "scalar", axis=2, tiled=True)
    fields_cols, velocity_cols = (
        lax.all_to_all(fields, "space", split_axis=3, concat_axis=2, tiled=True),
        lax.all_to_all(along_y[None], "space", split_axis=3, concat_axis=2, tiled=True),
    )
    remeshed = remesh_columns(fields_cols, velocity_cols[0], shift_y)
    returned = diffuse_columns(remeshed, diffusivity, tables_y)
    fields = lax.all_to_all(returned, "space", split_axis=2, concat_axis=3, tiled=True)
    along_x = fetch_velocity(velocity_x)
    return one_sweep(fields, along_x, shift_x, 0.5 * diffusivity, tables_x)


def solution(mesh):
    return jax.shard_map(
        on_device,
        mesh=mesh,
        in_specs=(
            P("scalar", None, "space", None),
            P(None, "space", "scalar"),
            P(None, "space", "scalar"),
            P(None, "space"),
            P("space"),
            P("scalar"),
        ),
        out_specs=P("scalar", None, "space", None),
        check_vma=False,
    )
```

profile of v0, /device:TPU:9, one launch (start us, length us, event | category | flops | bytes accessed | tf_op | source)
XLA Modules:
  0.0 666.9 jit_solution(6938982422818095112)
XLA Ops:
  13.6 24.2 %all-gather.3.cloned.1.call-done = f32[2,128,1024]{2,1,0:T(8,128)} async-done(((f32[2,128,256]{2,1,0:T(8,128)}), f32[2,128,1024]{2,1,0:T(8,128)}) %all-gather.3.cloned.1.call-update) | async-done | bytes 1048592 | tf_op jit(solution)/shard_map/all_gather | solution.py:99
  37.8 6.5 add_multiply_fusion.9
  44.3 6.1 broadcast_multiply_fusion.1
  57.6 8.0 %fusion.9 = f32[4,2,128,1024]{3,2,1,0:T(8,128)S(1)} fusion(f32[4,2,128,2]{3,2,1,0:T(8,128)S(1)} %slice.569, f32[4,2,128,1022]{3,2,1,0:T(8,128)} %slice.568, f32[4,2,128,1]{3,2,1,0:T(8,128)S(1)} %slice.571, f32[4,2,128,1023]{3,2,1,0:T(8,128)} %slice.570, f32[4,2,128,1023]{3,2,1,0:T(8,128)S(1)} %bitcast.156, f32[4,2,128,1]{3,2,1,0:T(8,128)S(1)} %slice.572, ...), kind=kLoop, calls=%fused_computation.16 | loop fusion | flops 11534336 | bytes 30408704 | tf_op jit(solution)/shard_map/add | solution.py:23
  79.8 4.8 fusion.262
  106.2 5.1 fusion.270
  116.0 26.6 %maximum_select_fusion.99 = f32[4,2,128,1024]{3,2,1,0:T(8,128)S(1)} fusion(f32[4,2,128,1016]{3,2,1,0:T(8,128)} %get-tuple-element.80, f32[4,2,128,8]{3,2,1,0:T(8,128)} %get-tuple-element.82, f32[4,2,128,1017]{3,2,1,0:T(8,128)} %get-tuple-element.84, f32[4,2,128,7]{3,2,1,0:T(8,128)} %get-tuple-element.86, ...), kind=kLoop, calls=%fused_computation.17.clone.clone.2 | loop fusion | flops 34603008 | bytes 75501824 | tf_op jit(solution)/shard_map/dot_general | solution.py:60
  142.7 32.3 %fusion.10 = f32[4,2,128,1024]{3,2,1,0:T(8,128)S(1)} fusion(s32[1024]{0:T(1024)S(1)} %copy-done.64, pred[1024]{0:T(1024)(128)(4,1)S(1)} %copy-done.67, f32[4,2,128,1024]{3,2,1,0:T(8,128)S(1)} %maximum_select_fusion.99), kind=kOutput, calls=%fused_computation.18 | convolution fusion | flops 12900630528 | bytes 8393728 | tf_op jit(solution)/shard_map/dot_general | solution.py:60
  175.9 32.3 %fusion.127 = f32[4,2,128,1024]{3,2,1,0:T(8,128)} fusion(f32[1024]{0:T(1024)S(1)} %copy-done.65, s32[1024]{0:T(1024)S(1)} %copy-done.64, pred[1024]{0:T(1024)(128)(4,1)S(1)} %copy-done.67, f32[4,2,128,1024]{3,2,1,0:T(8,128)S(1)} %fusion.301), kind=kOutput, calls=%fused_computation.181 | convolution fusion | flops 12901679104 | bytes 8397824 | tf_op jit(solution)/shard_map/dot_general | solution.py:65
  208.2 7.2 %copy.92 = f32[4,2,128,1024]{2,1,0,3:T(2,128)} copy(f32[4,2,128,1024]{3,2,1,0:T(8,128)} %fusion.127) | data formatting | bytes 8388608 | tf_op jit(solution)/shard_map/dot_general | solution.py:65
  220.1 6.2 subtract_maximum_fusion.11
  277.0 5.0 copy.93
  282.0 5.3 copy.94
  287.3 6.2 bitcast_multiply_fusion
  330.8 17.1 %maximum_select_fusion.100 = f32[4,2,1024,128]{3,2,1,0:T(8,128)S(1)} fusion(f32[4,2,1016,128]{3,2,1,0:T(8,128)} %get-tuple-element.43, f32[4,2,8,128]{3,2,1,0:T(8,128)S(1)} %get-tuple-element.45, f32[4,2,1017,128]{3,2,1,0:T(8,128)S(1)} %get-tuple-element.47, f32[4,2,7,128]{3,2,1,0:T(8,128)S(1)} %get-tuple-element.49, ...), kind=kLoop, calls=%fused_computation.72.clone.clone.2 | loop fusion | flops 34603008 | bytes 75499648 | tf_op jit(solution)/shard_map/jk,szjx->szkx/dot_general | solution.py:76
  347.9 44.4 %fusion.49 = f32[4,2,128,1024]{3,2,1,0:T(8,128)S(1)} fusion(s32[1024]{0:T(1024)S(1)} %copy-done.64, pred[1024]{0:T(1024)(128)(4,1)S(1)} %copy-done.67, f32[4,2,1024,128]{3,2,1,0:T(8,128)S(1)} %maximum_select_fusion.100), kind=kOutput, calls=%fused_computation.73 | convolution fusion | flops 12900630528 | bytes 8393728 | tf_op jit(solution)/shard_map/jk,szjx->szkx/dot_general | solution.py:76
  393.2 32.3 %fusion.142 = f32[4,2,1024,128]{2,3,1,0:T(8,128)} fusion(f32[1024]{0:T(1024)S(1)} %copy-done.65, s32[1024]{0:T(1024)S(1)} %copy-done.64, pred[1024]{0:T(1024)(128)(4,1)S(1)} %copy-done.67, f32[4,2,1024,128]{2,3,1,0:T(8,128)S(1)} %fusion.303), kind=kOutput, calls=%fused_computation.204 | convolution fusion | flops 12901679104 | bytes 8397824 | tf_op jit(solution)/shard_map/kj,szkx->szjx/dot_general | solution.py:85
  425.5 7.2 %copy.122 = f32[4,2,1024,128]{3,1,0,2:T(2,128)} copy(f32[4,2,1024,128]{2,3,1,0:T(8,128)} %fusion.142) | data formatting | bytes 8388608 | tf_op jit(solution)/shard_map/kj,szkx->szjx/transpose | solution.py:85
  432.8 51.9 %all_to_all.45 = f32[4,2,1024,128]{3,1,0,2:T(2,128)S(1)} all-to-all(f32[4,2,1024,128]{3,1,0,2:T(2,128)} %copy.122), channel_id=1, replica_groups=mesh['scalar'=4,'space'=8] {'space'}, dimensions={2} | all-to-all | bytes 8388608 | tf_op jit(solution)/shard_map/all_to_all | solution.py:115
  489.2 5.0 all_to_all.41
  494.1 5.6 broadcast_multiply_fusion
  510.1 8.3 %fusion.87 = f32[4,2,128,1024]{3,2,1,0:T(8,128)S(1)} fusion(f32[4,2,128,2]{3,2,1,0:T(8,128)} %slice.653, f32[4,2,128,1022]{3,2,1,0:T(8,128)} %slice.652, f32[4,2,128,1]{3,2,1,0:T(8,128)} %slice.655, f32[4,2,128,1023]{3,2,1,0:T(8,128)} %slice.654, f32[4,2,128,1023]{3,2,1,0:T(8,128)} %bitcast.154, f32[4,2,128,1]{3,2,1,0:T(8,128)S(1)} %slice.656, ...), kind=kLoop, calls=%fused_computation.126 | loop fusion | flops 11534336 | bytes 30408704 | tf_op jit(solution)/shard_map/add | solution.py:23
  522.0 4.9 fusion.234
  526.9 5.0 fusion.236
  531.9 4.8 fusion.238
  536.7 5.0 fusion.240
  541.7 4.9 fusion.242
  546.6 4.9 fusion.244
  551.5 5.0 fusion.230
  565.4 27.1 %maximum_select_fusion.101 = f32[4,2,128,1024]{3,2,1,0:T(8,128)} fusion(f32[4,2,128,1016]{3,2,1,0:T(8,128)} %get-tuple-element.6, f32[4,2,128,8]{3,2,1,0:T(8,128)} %get-tuple-element.8, f32[4,2,128,1017]{3,2,1,0:T(8,128)} %get-tuple-element.10, f32[4,2,128,7]{3,2,1,0:T(8,128)S(1)} %get-tuple-element.12, ...), kind=kLoop, calls=%fused_computation.127.clone.clone | loop fusion | flops 34603008 | bytes 75501824 | tf_op jit(solution)/shard_map/dot_general | solution.py:60
  592.5 34.5 %fusion.88 = f32[4,2,128,1024]{3,2,1,0:T(8,128)S(1)} fusion(s32[1024]{0:T(1024)S(1)} %copy-done.64, pred[1024]{0:T(1024)(128)(4,1)S(1)} %copy-done.67, f32[4,2,128,1024]{3,2,1,0:T(8,128)} %maximum_select_fusion.101), kind=kOutput, calls=%fused_computation.128 | convolution fusion | flops 12900630528 | bytes 8393728 | tf_op jit(solution)/shard_map/dot_general | solution.py:60
  627.9 32.0 %fusion.123 = f32[4,2,128,1024]{3,2,1,0:T(8,128)} fusion(f32[1024]{0:T(1024)S(1)} %copy-done.65, s32[1024]{0:T(1024)S(1)} %copy-done.64, pred[1024]{0:T(1024)(128)(4,1)S(1)} %copy-done.67, f32[4,2,128,1024]{3,2,1,0:T(8,128)S(1)} %fusion.299), kind=kOutput, calls=%fused_computation.177 | convolution fusion | flops 12901679104 | bytes 8397824 | tf_op jit(solution)/shard_map/dot_general | solution.py:65
  (241 shorter events, 176.3 us)
Async XLA Ops:
  6.5 31.3 %all-gather.3.cloned.1.call-start = ((), (), s32[]{:S(2)}) async-start(), calls=%async_computation.3 | async-start | bytes 1310720 | tf_op jit(solution)/shard_map/all_gather | solution.py:99
  7.3 104.0 %all-gather.5.cloned.1.call-start = ((), (), s32[]{:S(2)}) async-start(), calls=%async_computation.4 | async-start | bytes 1310720 | tf_op jit(solution)/shard_map/all_gather | solution.py:108
  12.1 103.7 %copy-start.30 = (pred[2,128]{1,0:T(4,128)(4,1)}, pred[2,128]{1,0:T(4,128)(4,1)S(1)}, u32[]{:S(2)}) copy-start(pred[2,128]{1,0:T(4,128)(4,1)S(1)} %get-tuple-element.142) | copy-start | bytes 772
  12.1 103.7 %copy-start.32 = (pred[2,128]{1,0:T(4,128)(4,1)}, pred[2,128]{1,0:T(4,128)(4,1)S(1)}, u32[]{:S(2)}) copy-start(pred[2,128]{1,0:T(4,128)(4,1)S(1)} %get-tuple-element.143) | copy-start | bytes 772
  12.1 103.7 %copy-start.34 = (pred[2,128]{1,0:T(4,128)(4,1)}, pred[2,128]{1,0:T(4,128)(4,1)S(1)}, u32[]{:S(2)}) copy-start(pred[2,128]{1,0:T(4,128)(4,1)S(1)} %get-tuple-element.144) | copy-start | bytes 772
  12.1 103.7 %copy-start.36 = (pred[2,128]{1,0:T(4,128)(4,1)}, pred[2,128]{1,0:T(4,128)(4,1)S(1)}, u32[]{:S(2)}) copy-start(pred[2,128]{1,0:T(4,128)(4,1)S(1)} %get-tuple-element.145) | copy-start | bytes 772
  12.1 103.7 %copy-start.38 = (pred[2,128]{1,0:T(4,128)(4,1)}, pred[2,128]{1,0:T(4,128)(4,1)S(1)}, u32[]{:S(2)}) copy-start(pred[2,128]{1,0:T(4,128)(4,1)S(1)} %get-tuple-element.146) | copy-start | bytes 772
  12.2 103.7 %copy-start.40 = (pred[2,128]{1,0:T(4,128)(4,1)}, pred[2,128]{1,0:T(4,128)(4,1)S(1)}, u32[]{:S(2)}) copy-start(pred[2,128]{1,0:T(4,128)(4,1)S(1)} %get-tuple-element.147) | copy-start | bytes 772
  12.2 103.7 %copy-start.42 = (pred[2,128]{1,0:T(4,128)(4,1)}, pred[2,128]{1,0:T(4,128)(4,1)S(1)}, u32[]{:S(2)}) copy-start(pred[2,128]{1,0:T(4,128)(4,1)S(1)} %get-tuple-element.148) | copy-start | bytes 772
  12.2 103.7 %copy-start.44 = (pred[2,128]{1,0:T(4,128)(4,1)}, pred[2,128]{1,0:T(4,128)(4,1)S(1)}, u32[]{:S(2)}) copy-start(pred[2,128]{1,0:T(4,128)(4,1)S(1)} %get-tuple-element.149) | copy-start | bytes 772
  12.2 103.7 %copy-start.46 = (pred[2,128]{1,0:T(4,128)(4,1)}, pred[2,128]{1,0:T(4,128)(4,1)S(1)}, u32[]{:S(2)}) copy-start(pred[2,128]{1,0:T(4,128)(4,1)S(1)} %get-tuple-element.150) | copy-start | bytes 772
  12.2 103.7 %copy-start.48 = (pred[2,128]{1,0:T(4,128)(4,1)}, pred[2,128]{1,0:T(4,128)(4,1)S(1)}, u32[]{:S(2)}) copy-start(pred[2,128]{1,0:T(4,128)(4,1)S(1)} %get-tuple-element.151) | copy-start | bytes 772
  12.2 103.7 %copy-start.50 = (pred[2,128]{1,0:T(4,128)(4,1)}, pred[2,128]{1,0:T(4,128)(4,1)S(1)}, u32[]{:S(2)}) copy-start(pred[2,128]{1,0:T(4,128)(4,1)S(1)} %get-tuple-element.152) | copy-start | bytes 772
  12.2 103.7 %copy-start.52 = (pred[2,128]{1,0:T(4,128)(4,1)}, pred[2,128]{1,0:T(4,128)(4,1)S(1)}, u32[]{:S(2)}) copy-start(pred[2,128]{1,0:T(4,128)(4,1)S(1)} %get-tuple-element.153) | copy-start | bytes 772
  12.2 103.7 %copy-start.54 = (pred[2,128]{1,0:T(4,128)(4,1)}, pred[2,128]{1,0:T(4,128)(4,1)S(1)}, u32[]{:S(2)}) copy-start(pred[2,128]{1,0:T(4,128)(4,1)S(1)} %get-tuple-element.154) | copy-start | bytes 772
  13.6 161.4 %copy-start.27 = (f32[4,1024]{1,0:T(4,128)}, f32[4,1024]{1,0:T(4,128)S(1)}, u32[]{:S(2)}) copy-start(f32[4,1024]{1,0:T(4,128)S(1)} %get-tuple-element.141) | copy-start | bytes 49156
  44.3 13.3 %copy-start.4 = (f32[2,128,1024]{2,1,0:T(8,128)}, f32[2,128,1024]{2,1,0:T(8,128)S(1)}, u32[]{:S(2)}) copy-start(f32[2,128,1024]{2,1,0:T(8,128)S(1)} %get-tuple-element.134) | copy-start | bytes 3145732
  65.6 40.6 %copy-start = (f32[4,2,128,1024]{3,2,1,0:T(8,128)}, f32[4,2,128,1024]{3,2,1,0:T(8,128)S(1)}, u32[]{:S(2)}) copy-start(f32[4,2,128,1024]{3,2,1,0:T(8,128)S(1)} %fusion.9) | copy-start | bytes 12582916
  106.2 9.7 %copy-start.56 = (pred[2,128]{1,0:T(4,128)(4,1)S(1)}, pred[2,128]{1,0:T(4,128)(4,1)}, u32[]{:S(2)}) copy-start(pred[2,128]{1,0:T(4,128)(4,1)} %get-tuple-element.155) | copy-start | bytes 772
  106.2 9.7 %copy-start.58 = (pred[2,128]{1,0:T(4,128)(4,1)S(1)}, pred[2,128]{1,0:T(4,128)(4,1)}, u32[]{:S(2)}) copy-start(pred[2,128]{1,0:T(4,128)(4,1)} %get-tuple-element.156) | copy-start | bytes 772
  106.2 9.8 %copy-start.60 = (pred[2,128]{1,0:T(4,128)(4,1)S(1)}, pred[2,128]{1,0:T(4,128)(4,1)}, u32[]{:S(2)}) copy-start(pred[2,128]{1,0:T(4,128)(4,1)} %get-tuple-element.157) | copy-start | bytes 772
  106.2 9.8 %copy-start.62 = (pred[2,128]{1,0:T(4,128)(4,1)S(1)}, pred[2,128]{1,0:T(4,128)(4,1)}, u32[]{:S(2)}) copy-start(pred[2,128]{1,0:T(4,128)(4,1)} %get-tuple-element.158) | copy-start | bytes 772
  111.3 104.2 %all-to-all-start.1 = ((f32[1,2,128,1024]{2,1,0,3:T(2,128)}), f32[1,2,128,1024]{2,1,0,3:T(2,128)S(1)}, u32[]{:S(2)}, u32[]{:S(2)}) async-start(f32[1,2,128,1024]{2,1,0,3:T(2,128)} %bitcast.199), calls=%async_computation.1 | async-start | bytes 2097152 | tf_op jit(solution)/shard_map/all_to_all | solution.py:111
  116.0 26.7 %copy-start.64 = (s32[1024]{0:T(1024)S(1)}, s32[1024]{0:T(1024)}, u32[]{:S(2)}) copy-start(s32[1024]{0:T(1024)} %add_select_fusion.2) | copy-start | bytes 12292
  116.0 26.7 %copy-start.67 = (pred[1024]{0:T(1024)(128)(4,1)S(1)}, pred[1024]{0:T(1024)(128)(4,1)}, u32[]{:S(2)}) copy-start(pred[1024]{0:T(1024)(128)(4,1)} %iota_compare_fusion.1) | copy-start | bytes 3076
  215.5 61.5 %all-to-all-start = ((f32[4,2,128,1024]{2,1,0,3:T(2,128)}), f32[4,2,128,1024]{2,1,0,3:T(2,128)}, u32[]{:S(2)}, u32[]{:S(2)}) async-start(f32[4,2,128,1024]{2,1,0,3:T(2,128)} %copy.92), calls=%async_computation | async-start | bytes 8388608 | tf_op jit(solution)/shard_map/all_to_all | solution.py:110
  228.9 10.3 %copy-start.11 = (f32[1,2,128,1024]{2,3,1,0:T(8,128)S(1)}, f32[1,2,128,1024]{2,3,1,0:T(8,128)}, u32[]{:S(2)}) copy-start(f32[1,2,128,1024]{2,3,1,0:T(8,128)} %get-tuple-element.121) | copy-start | bytes 3145732
  240.6 10.3 %copy-start.10 = (f32[1,2,128,1024]{2,3,1,0:T(8,128)S(1)}, f32[1,2,128,1024]{2,3,1,0:T(8,128)}, u32[]{:S(2)}) copy-start(f32[1,2,128,1024]{2,3,1,0:T(8,128)} %get-tuple-element.127) | copy-start | bytes 3145732
  252.2 10.3 %copy-start.9 = (f32[1,2,128,1024]{2,3,1,0:T(8,128)S(1)}, f32[1,2,128,1024]{2,3,1,0:T(8,128)}, u32[]{:S(2)}) copy-start(f32[1,2,128,1024]{2,3,1,0:T(8,128)} %get-tuple-element.116) | copy-start | bytes 3145732
  347.9 44.4 %copy-start.29 = (f32[4,1024]{1,0:T(4,128)S(1)}, f32[4,1024]{1,0:T(4,128)}, u32[]{:S(2)}) copy-start(f32[4,1024]{1,0:T(4,128)} %get-tuple-element.140) | copy-start | bytes 49156
  503.8 6.3 copy-start.5
  592.5 34.6 %copy-start.28 = (f32[4,1024]{1,0:T(4,128)S(1)}, f32[4,1024]{1,0:T(4,128)}, u32[]{:S(2)}) copy-start(f32[4,1024]{1,0:T(4,128)} %copy-done.27) | copy-start | bytes 49156
  (40 other events, 169.0 us)
Sparse Core Ops, SparseCore 0:
  8.9 28.8 all-gather.2
  39.4 27.4 all-gather.4
where the time goes:
time: 677 us; the launch traced here: 667 us
  local copies, waits for them, and re-layouts  219 us (32%)
  matrix products  208 us (31%)
  other arithmetic  139 us (21%)
  blocking collectives  51.9 us (8%)
  waiting for transfers between devices  24.9 us (4%)
  between operations  14.6 us (2%)
  starting transfers between devices  9.21 us (1%)
    slice x32, local copies, waits for them, and re-layouts, remesh(): jnp.roll(summed, amount, axis=-1)  92.3 us
    dot_general x2, matrix products, diffuse(): jnp.dot(rows_flat, forward, precision=lax.Precision.HIGHEST, preferred_el...  66.9 us
    dot_general x2, matrix products, diffuse(): jnp.dot(spectra.reshape(-1, initial[-1]), inverse, precision=lax.Precisio...  64.3 us
    dot_general x2, other arithmetic, diffuse(): jnp.dot(rows_flat, forward, precision=lax.Precision.HIGHEST, preferred_el...  53.8 us
    all_to_all x1, blocking collectives, on_device(): lax.all_to_all(returned, 'space', split_axis=2, concat_axis=3, tiled=True)  51.9 us
    dot_general x1, matrix products, diffuse_columns(): jnp.einsum('jk,szjx->szkx', forward, fields, precision=lax.Precision.HIGH...  44.4 us
    dot_general x1, matrix products, diffuse_columns(): jnp.einsum('kj,szkx->szjx', inverse, spectra, precision=lax.Precision.HIG...  32.3 us
    slice x16, local copies, waits for them, and re-layouts, remesh_columns(): jnp.roll(summed, amount, axis=2)  25.1 us
  transfers between devices with their start and end apart: 4, of which 1 were waited for; matrix products, arithmetic and copies ran while one was open for 35% of the time, Pallas kernels for 0%

commit v1 on v0

--- a/solution.py
+++ b/solution.py
@@ -1,8 +1,12 @@
+import functools
 import math
 
 import jax
 import jax.numpy as jnp
+import numpy as np
 from jax import lax
+from jax.experimental import pallas as pl
+from jax.experimental.pallas import tpu as pltpu
 from jax.sharding import PartitionSpec as P
 
 NY = 1024
@@ -117,9 +121,298 @@
     return one_sweep(fields, along_x, shift_x, 0.5 * diffusivity, tables_x)
 
 
+BLOCK = 256
+REACH = 8
+MESH = pl.DeviceIdType.MESH
+
+
+def spline_weights(f):
+    g = 1.0 - f
+
+    def fifth(v):
+        w = v * v
+        return w * w * v
+
+    f0, f1, f2 = fifth(f), fifth(1.0 + f), fifth(2.0 + f)
+    g0, g1, g2 = fifth(g), fifth(1.0 + g), fifth(2.0 + g)
+    c = 1.0 / 120.0
+    return (
+        g0 * c,
+        (g1 - 6.0 * g0) * c,
+        (g2 - 6.0 * g1 + 15.0 * g0) * c,
+        (f2 - 6.0 * f1 + 15.0 * f0) * c,
+        (f1 - 6.0 * f0) * c,
+        f0 * c,
+    )
+
+
+def response(kappa, length):
+    half = length // 2
+    k = np.arange(half + 1)
+    weight = np.where((k == 0) | (k == half), 1.0, 2.0) / length
+    phase = (k[:, None] * np.arange(length)[None, :]) % length
+    table = (np.cos(phase * (2.0 * np.pi / length)) * weight[:, None]).astype(np.float32)
+    relative = jnp.arange(half + 1).astype(jnp.float32) / half
+    damping = jnp.exp(-kappa[:, None] * relative * relative)
+    return jnp.dot(damping, table, precision=lax.Precision.HIGHEST, preferred_element_type=jnp.float32)
+
+
+def circulant_kernel(g_ref, hi_ref, lo_ref):
+    length = g_ref.shape[-1]
+    wide = jnp.broadcast_to(g_ref[0], (BLOCK, length))
+    turned = pltpu.roll(wide, 0, 1, stride=1, stride_axis=0)
+    high = turned.astype(jnp.bfloat16)
+    hi_ref[0] = high
+    lo_ref[0] = (turned - high.astype(jnp.float32)).astype(jnp.bfloat16)
+
+
+def circulant_blocks(g):
+    count, length = g.shape
+    spec = pl.BlockSpec((1, BLOCK, length), lambda i: (i, 0, 0))
+    return pl.pallas_call(
+        circulant_kernel,
+        grid=(count,),
+        in_specs=[pl.BlockSpec((1, 1, length), lambda i: (i, 0, 0))],
+        out_specs=[spec, spec],
+        out_shape=[jax.ShapeDtypeStruct((count, BLOCK, length), jnp.bfloat16)] * 2,
+    )(g[:, None, :])
+
+
+def halves(v):
+    high = v.astype(jnp.bfloat16)
+    return high, (v - high.astype(jnp.float32)).astype(jnp.bfloat16)
+
+
+def dot32(a, b):
+    return jnp.dot(a, b, preferred_element_type=jnp.float32)
+
+
+def sweeps_kernel(
+    peers,
+    q_ref, vx_ref, vy_ref, sx_ref, sy_ref, xh_ref, xl_ref, yh_ref, yl_ref,
+    out_ref,
+    wx, wy, part_hi, part_lo, swept, col_hi, col_lo, tall,
+    ext, cols, turned, back,
+    send1, recv1, send2, recv2,
+):
+    ns, nz, rows, nx = q_ref.shape
+    ny = rows * peers
+    width = nx // peers
+    me = lax.axis_index("space")
+    bx, by = nx // BLOCK, ny // BLOCK
+
+    barrier = pltpu.get_barrier_semaphore()
+    for k in range(1, peers):
+        pl.semaphore_signal(barrier, inc=1, device_id={"space": lax.rem(me + k, peers)}, device_id_type=MESH)
+
+    step = 16
+    per = rows // step
+
+    @pl.loop(0, nz * per)
+    def _(i):
+        z, r = i // per, pl.multiple_of((i % per) * step, step)
+        for v_ref, w_ref in ((vx_ref, wx), (vy_ref, wy)):
+            for m, w in enumerate(spline_weights(v_ref[z, pl.ds(r, step), :])):
+                w_ref[z, m, pl.ds(r, step), :] = w
+
+    def remesh_rows(load):
+        @pl.loop(0, nz * per)
+        def _(i):
+            z, r = i // per, pl.multiple_of((i % per) * step, step)
+            q = load(z, r)
+            acc = q * wx[z, 5, pl.ds(r, step), :]
+            for m in range(4, -1, -1):
+                acc = pltpu.roll(acc, 1, 1) + q * wx[z, m, pl.ds(r, step), :]
+            shift = sx_ref[z, pl.ds(r, step), :] + REACH
+            for bit in (1, 2, 4, 8, 16):
+                acc = jnp.where((shift & bit) != 0, pltpu.roll(acc, bit, 1), acc)
+            at = pl.multiple_of(z * rows + r, step)
+            part_hi[pl.ds(at, step), :], part_lo[pl.ds(at, step), :] = halves(acc)
+
+    def diffuse_rows(s, store):
+        for b in range(bx):
+            total = jnp.zeros((nz * rows, BLOCK), jnp.float32)
+            for a in range(bx):
+                d = ((b - a) % bx) * BLOCK
+                high, low = xh_ref[s, :, d:d + BLOCK], xl_ref[s, :, d:d + BLOCK]
+                left = part_hi[:, a * BLOCK:(a + 1) * BLOCK]
+                rest = part_lo[:, a * BLOCK:(a + 1) * BLOCK]
+                total = total + (dot32(left, high) + (dot32(left, low) + dot32(rest, high)))
+            store(b * BLOCK, total)
+
+    def forward(s, k):
+        dest = lax.rem(me + k, peers)
+        return pltpu.make_async_remote_copy(
+            src_ref=ext.at[s, dest], dst_ref=cols.at[s, me],
+            send_sem=send1.at[s, k - 1], recv_sem=recv1.at[s, k - 1],
+            device_id={"space": dest}, device_id_type=MESH,
+        )
+
+    def backward(s, k):
+        dest = lax.rem(me + k, peers)
+        return pltpu.make_async_remote_copy(
+            src_ref=turned.at[s, dest], dst_ref=back.at[s, me],
+            send_sem=send2.at[s, k - 1], recv_sem=recv2.at[s, k - 1],
+            device_id={"space": dest}, device_id_type=MESH,
+        )
+
+    edge = lax.broadcasted_iota(jnp.int32, (8, width), 0)
+
+    def first(s):
+        remesh_rows(lambda z, r: q_ref[s, z, pl.ds(r, step), :])
+
+        def store(c, total):
+            swept[:, c:c + BLOCK] = total
+
+        diffuse_rows(s, store)
+
+        @pl.loop(0, nz * peers)
+        def _(i):
+            p, z = i // nz, i % nz
+            lanes = pl.ds(pl.multiple_of(p * width, width), width)
+            y = swept[pl.ds(pl.multiple_of(z * rows, rows), rows), lanes]
+            pad = jnp.zeros((8, width), jnp.float32)
+            acc = jnp.zeros((rows + 16, width), jnp.float32)
+            for m in range(-2, 4):
+                term = jnp.concatenate([pad, y * wy[z, m + 2, :, lanes], pad], axis=0)
+                acc = acc + (term if m == 0 else pltpu.roll(term, m % (rows + 16), 0))
+            ext[s, p, z, 0:rows, :] = acc[8:8 + rows]
+            ext[s, p, z, rows:rows + 8, :] = jnp.where(edge < 3, acc[rows + 8:], acc[:8])
+
+        cols[s, me] = ext[s, me]
+
+    @pl.loop(0, 1)
+    def _(s):
+        first(s)
+
+    pl.semaphore_wait(barrier, peers - 1)
+    for k in range(1, peers):
+        forward(0, k).start()
+
+    @pl.loop(1, ns)
+    def _(s):
+        first(s)
+        for k in range(1, peers):
+            forward(s, k).start()
+
+    @pl.loop(0, ns)
+    def _(s):
+        for k in range(1, peers):
+            forward(s, k).wait_recv()
+
+        for p in range(peers):
+            for z in range(nz):
+                lanes = slice(z * width, (z + 1) * width)
+                top = jnp.where(edge < 3, cols[s, (p - 1) % peers, z, rows:rows + 8, :], 0.0)
+                low = jnp.where(edge >= 6, cols[s, (p + 1) % peers, z, rows:rows + 8, :], 0.0)
+                at = 8 + p * rows
+                tall[at:at + 8, lanes] = cols[s, p, z, 0:8, :] + top
+                tall[at + 8:at + rows - 8, lanes] = cols[s, p, z, 8:rows - 8, :]
+                tall[at + rows - 8:at + rows, lanes] = cols[s, p, z, rows - 8:rows, :] + low
+        tall[0:8, :] = tall[ny:ny + 8, :]
+        tall[ny + 8:ny + 16, :] = tall[8:16, :]
+
+        @pl.loop(0, peers)
+        def _(p):
+            at = pl.multiple_of(p * rows, rows)
+            ahead = REACH - sy_ref[...]
+            for z in range(nz):
+                lanes = slice(z * width, (z + 1) * width)
+                u = tall[pl.ds(at, rows + 16), lanes]
+                for bit in (1, 2, 4, 8, 16):
+                    u = jnp.where((ahead & bit) != 0, pltpu.roll(u, rows + 16 - bit, 0), u)
+                col_hi[pl.ds(at, rows), lanes], col_lo[pl.ds(at, rows), lanes] = halves(u[:rows])
+
+        for a in range(by):
+            total = jnp.zeros((BLOCK, nz * width), jnp.float32)
+            for b in range(by):
+                d = ((b - a) % by) * BLOCK
+                high, low = yh_ref[s, :, d:d + BLOCK], yl_ref[s, :, d:d + BLOCK]
+                left = col_hi[b * BLOCK:(b + 1) * BLOCK, :]
+                rest = col_lo[b * BLOCK:(b + 1) * BLOCK, :]
+                total = total + (dot32(high, left) + (dot32(low, left) + dot32(high, rest)))
+            for h in range(BLOCK // rows):
+                for z in range(nz):
+                    turned[s, a * (BLOCK // rows) + h, z] = total[
+                        h * rows:(h + 1) * rows, z * width:(z + 1) * width
+                    ]
+        back[s, me] = turned[s, me]
+        for k in range(1, peers):
+            backward(s, k).start()
+
+    @pl.loop(0, ns)
+    def _(s):
+        for k in range(1, peers):
+            backward(s, k).wait_recv()
+        remesh_rows(
+            lambda z, r: jnp.concatenate(
+                [back[s, p, z, pl.ds(r, step), :] for p in range(peers)], axis=1
+            )
+        )
+
+        def store(c, total):
+            for z in range(nz):
+                out_ref[s, z, :, c:c + BLOCK] = total[z * rows:(z + 1) * rows]
+
+        diffuse_rows(s, store)
+
+    @pl.loop(0, ns)
+    def _(s):
+        for k in range(1, peers):
+            forward(s, k).wait_send()
+            backward(s, k).wait_send()
+
+
+def sweeps_on_device(peers, scalars, velocity_x, velocity_y, shift_x, shift_y, schmidt):
+    ns, nz, rows, nx = scalars.shape
+    ny, width = rows * peers, nx // peers
+    along_x = fetch_velocity(velocity_x)
+    along_y = fetch_velocity(velocity_y)
+    diffusivity = jnp.exp2((3 - schmidt).astype(jnp.float32))
+    line_x = jnp.roll(response(0.5 * diffusivity, nx), -(REACH + 2), axis=1)
+    line_y = response(diffusivity, ny)
+    xh, xl = circulant_blocks(line_x)
+    yh, yl = circulant_blocks(line_y)
+    f32, bf16 = jnp.float32, jnp.bfloat16
+    vmem = pl.BlockSpec(memory_space=pltpu.VMEM)
+    dma = pltpu.SemaphoreType.DMA((ns, peers - 1))
+    return pl.pallas_call(
+        functools.partial(sweeps_kernel, peers),
+        out_shape=jax.ShapeDtypeStruct(scalars.shape, f32),
+        in_specs=[vmem] * 9,
+        out_specs=vmem,
+        scratch_shapes=[
+            pltpu.VMEM((nz, 6, rows, nx), f32),
+            pltpu.VMEM((nz, 6, rows, nx), f32),
+            pltpu.VMEM((nz * rows, nx), bf16),
+            pltpu.VMEM((nz * rows, nx), bf16),
+            pltpu.VMEM((nz * rows, nx), f32),
+            pltpu.VMEM((ny, nz * width), bf16),
+            pltpu.VMEM((ny, nz * width), bf16),
+            pltpu.VMEM((ny + 16, nz * width), f32),
+            pltpu.VMEM((ns, peers, nz, rows + 8, width), f32),
+            pltpu.VMEM((ns, peers, nz, rows + 8, width), f32),
+            pltpu.VMEM((ns, peers, nz, rows, width), f32),
+            pltpu.VMEM((ns, peers, nz, rows, width), f32),
+            dma, dma, dma, dma,
+        ],
+        compiler_params=pltpu.CompilerParams(
+            collective_id=0, has_side_effects=True, vmem_limit_bytes=62 * 2**20
+        ),
+    )(
+        scalars, along_x, along_y, shift_x[:, :, None], shift_y[None, :], xh, xl, yh, yl
+    )
+
+
+def fits_kernel(mesh):
+    return NY % mesh.shape["space"] == 0 and NY // mesh.shape["space"] in (128, 256)
+
+
 def solution(mesh):
+    peers = mesh.shape["space"]
+    body = functools.partial(sweeps_on_device, peers) if fits_kernel(mesh) else on_device
     return jax.shard_map(
-        on_device,
+        body,
         mesh=mesh,
         in_specs=(
             P("scalar", None, "space", None),

time: 677 us -> 249 us (0.37); the launches traced: 667 us -> 247 us
  local copies, waits for them, and re-layouts: 219 us -> 6.93 us
  matrix products: 208 us -> 3.95 us
  Pallas kernels: 0 us -> 176 us
  other arithmetic: 139 us -> 0.75 us
  blocking collectives: 51.9 us -> 0 us
  waiting for transfers between devices: 24.9 us -> 45.9 us
  starting transfers between devices: 9.21 us -> 0.04 us
    dot_general x6 -> x2, matrix products: 208 us -> 3.95 us  [response(): jnp.dot(damping, table, precision=lax.Precision.HIGHEST, preferred_elemen...]
    pallas_call x0 -> x3, Pallas kernels: none -> 176 us  [the longest x1 169 us: sweeps_on_device(): pl.pallas_call(functools.partial(sweeps_kernel, peers), out_shape=jax.Sha...]
    slice x69 -> x2, local copies, waits for them, and re-layouts: 140 us -> 0.08 us  [sweeps_on_device(): line_x = jnp.roll(response(0.5 * diffusivity, nx), -(REACH + 2), axis=1)]
    dot_general x6 -> x0, other arithmetic: 73.4 us -> none  [the longest x2 53.8 us: diffuse(): jnp.dot(rows_flat, forward, precision=lax.Precision.HIGHEST, preferred_el...]
    all_to_all x1 -> x0, blocking collectives: 51.9 us -> none  [on_device(): lax.all_to_all(returned, 'space', split_axis=2, concat_axis=3, tiled=True)]
    max x18 -> x0, local copies, waits for them, and re-layouts: 40.1 us -> none  [the longest x6 14.1 us: spline(): far_part = jnp.maximum(3.0 - magnitude, 0.0)]
    add x3 -> x0, other arithmetic: 20.9 us -> none  [the longest x2 16.3 us: remesh(): summed = summed + jnp.roll(fields * weight, offset, axis=-1)]
    all_gather x1 -> x2, waiting for transfers between devices: 24.2 us -> 44.5 us  [fetch_velocity(): return lax.all_gather(velocity_x, 'scalar', axis=2, tiled=True)]
  transfers between devices with their start and end apart: 4 -> 2, of which waited for: 1 -> 2; matrix products, arithmetic and copies ran while one was open for 35% -> 3% of each run, Pallas kernels for 0% -> 3%
where the time goes in v1:
time: 249 us; the launch traced here: 247 us
  Pallas kernels  176 us (71%)
  waiting for transfers between devices  45.9 us (18%)
  between operations  13.4 us (5%)
  local copies, waits for them, and re-layouts  6.93 us (3%)
  matrix products  3.95 us (2%)
    pallas_call x1, Pallas kernels, sweeps_on_device(): pl.pallas_call(functools.partial(sweeps_kernel, peers), out_shape=jax.Sha...  169 us
    all_gather x2, waiting for transfers between devices, fetch_velocity(): return lax.all_gather(velocity_x, 'scalar', axis=2, tiled=True)  44.5 us
    pallas_call x2, Pallas kernels, circulant_blocks(): pl.pallas_call(circulant_kernel, grid=(count,), in_specs=[pl.BlockSpec((1...  7.5 us
  transfers between devices with their start and end apart: 2, of which 2 were waited for; matrix products, arithmetic and copies ran while one was open for 3% of the time, Pallas kernels for 3%

profile of v1, /device:TPU:9, one launch (start us, length us, event | category | flops | bytes accessed | tf_op | source)
XLA Modules:
  0.0 247.4 jit_solution(9945706101983715000)
XLA Ops:
  6.5 0.0 copy-start
  6.5 0.0 all-gather.3.cloned.1.call-start
  6.5 0.7 all-gather.3.cloned.1.call-update
  7.3 0.0 all-gather.5.cloned.1.call-start
  7.3 0.7 all-gather.5.cloned.1.call-update
  8.0 0.7 fusion.6
  8.7 0.0 copy-start.1
  8.7 2.8 %fusion = f32[4,1024]{1,0:T(4,128)S(1)} fusion(f32[513,1024]{1,0:T(8,128)} %constant.11.clone, f32[513]{0:T(1024)S(1)} %convert_multiply_fusion, f32[4]{0:T(128)S(1)} %get-tuple-element.14), kind=kOutput, calls=%fused_computation.3 | convolution fusion | flops 25219080 | bytes 2119700 | tf_op jit(solution)/shard_map/dot_general | solution.py:157
  11.5 0.1 slice.10
  11.5 0.1 pad_maximum_fusion
  11.6 0.6 broadcast_in_dim.20.g_ref
  12.3 0.0 copy-done
  12.3 1.2 fusion.1
  13.4 0.6 broadcast_in_dim.21.g_ref
  14.1 0.0 copy-done.1
  14.1 0.8 copy.9.sx_ref
  14.9 3.8 %shard_map.83 = (bf16[4,256,1024]{2,1,0:T(8,128)(2,1)}, bf16[4,256,1024]{2,1,0:T(8,128)(2,1)}) custom-call(f32[4,1,1024]{2,1,0:T(1,128)} %broadcast_in_dim.21.g_ref), custom_call_target="tpu_custom_call" | custom-call | tf_op jit(solution)/shard_map/pallas_call | solution.py:172
  18.6 3.7 %shard_map.82 = (bf16[4,256,1024]{2,1,0:T(8,128)(2,1)}, bf16[4,256,1024]{2,1,0:T(8,128)(2,1)}) custom-call(f32[4,1,1024]{2,1,0:T(1,128)} %broadcast_in_dim.20.g_ref), custom_call_target="tpu_custom_call" | custom-call | tf_op jit(solution)/shard_map/pallas_call | solution.py:172
  22.4 15.4 %all-gather.3.cloned.1.call-done.vx_ref = f32[2,128,1024]{2,1,0:T(8,128)} async-done(((f32[2,128,256]{2,1,0:T(8,128)}), f32[2,128,1024]{2,1,0:T(8,128)}) %all-gather.3.cloned.1.call-update) | async-done | bytes 1048592 | tf_op jit(solution)/shard_map/all_gather | solution.py:103
  37.8 29.0 %all-gather.5.cloned.1.call-done.vy_ref = f32[2,128,1024]{2,1,0:T(8,128)} async-done(((f32[2,128,256]{2,1,0:T(8,128)}), f32[2,128,1024]{2,1,0:T(8,128)}) %all-gather.5.cloned.1.call-update) | async-done | bytes 1048592 | tf_op jit(solution)/shard_map/all_gather | solution.py:103
  66.8 169.0 %shard_map.84 = f32[4,2,128,1024]{3,2,1,0:T(8,128)} custom-call(f32[4,2,128,1024]{3,2,1,0:T(8,128)} %q_ref.1, f32[2,128,1024]{2,1,0:T(8,128)} %all-gather.3.cloned.1.call-done.vx_ref, f32[2,128,1024]{2,1,0:T(8,128)} %all-gather.5.cloned.1.call-done.vy_ref, s32[2,128,1]{2,1,0:T(8,128)} %copy.9.sx_ref, s32[1,128]{1,0:T(1,128)} %bitcast.5, ...), custom_call_target="tpu_custom_call" | custom-call | tf_op jit(solution)/shard_map/pallas_call | solution.py:379
  235.8 4.8 %copy.11 = f32[4,2,128,1024]{3,2,1,0:T(8,128)} copy(f32[4,2,128,1024]{3,2,1,0:T(8,128)} %shard_map.84) | data formatting | bytes 8388608
  (2 shorter events, 0.0 us)
Async XLA Ops:
  6.5 5.7 %copy-start = (f32[513,1024]{1,0:T(8,128)S(1)}, f32[513,1024]{1,0:T(8,128)}, u32[]{:S(2)}) copy-start(f32[513,1024]{1,0:T(8,128)} %constant.11.clone) | copy-start | bytes 6303748
  6.5 31.3 %all-gather.3.cloned.1.call-start = ((), (), s32[]{:S(2)}) async-start(), calls=%async_computation | async-start | bytes 1310720 | tf_op jit(solution)/shard_map/all_gather | solution.py:103
  7.3 59.6 %all-gather.5.cloned.1.call-start = ((), (), s32[]{:S(2)}) async-start(), calls=%async_computation.1 | async-start | bytes 1310720 | tf_op jit(solution)/shard_map/all_gather | solution.py:103
  8.7 5.4 %copy-start.1 = (s32[2,128]{1,0:T(2,128)S(1)}, s32[2,128]{1,0:T(2,128)}, u32[]{:S(2)}) copy-start(s32[2,128]{1,0:T(2,128)} %param.11) | copy-start | bytes 3076
Sparse Core Ops, SparseCore 0:
  8.9 28.8 all-gather.2
  39.4 27.4 all-gather.4

commit v2 on v1

--- a/solution.py
+++ b/solution.py
@@ -216,16 +216,18 @@
                 w_ref[z, m, pl.ds(r, step), :] = w
 
     def remesh_rows(load):
-        @pl.loop(0, nz * per)
+        @pl.loop(0, nz * per, unroll=2)
         def _(i):
             z, r = i // per, pl.multiple_of((i % per) * step, step)
             q = load(z, r)
-            acc = q * wx[z, 5, pl.ds(r, step), :]
-            for m in range(4, -1, -1):
-                acc = pltpu.roll(acc, 1, 1) + q * wx[z, m, pl.ds(r, step), :]
+            acc = q * wx[z, 0, pl.ds(r, step), :]
+            for m in range(1, 6):
+                acc = acc + pltpu.roll(q * wx[z, m, pl.ds(r, step), :], m, 1)
             shift = sx_ref[z, pl.ds(r, step), :] + REACH
-            for bit in (1, 2, 4, 8, 16):
-                acc = jnp.where((shift & bit) != 0, pltpu.roll(acc, bit, 1), acc)
+            for places, low in (((1, 2, 3), 3), ((4, 8, 12, 16), 28)):
+                now, base = shift & low, acc
+                for place in places:
+                    acc = jnp.where(now == place, pltpu.roll(base, place, 1), acc)
             at = pl.multiple_of(z * rows + r, step)
             part_hi[pl.ds(at, step), :], part_lo[pl.ds(at, step), :] = halves(acc)
 

time: 249 us -> 204 us (0.82)
  Pallas kernels: 176 us -> 132 us
    pallas_call x1, Pallas kernels: 169 us -> 124 us  [sweeps_on_device(): pl.pallas_call(functools.partial(sweeps_kernel, peers), out_shape=jax.Sha...]
  transfers between devices with their start and end apart: 2 -> 2, of which waited for: 2 -> 2; matrix products, arithmetic and copies ran while one was open for 3% -> 3% of each run, Pallas kernels for 3% -> 4%
where the time goes in v2:
time: 204 us; the launch traced here: 203 us
  Pallas kernels  132 us (65%)
  waiting for transfers between devices  45.9 us (22%)
  between operations  13.4 us (7%)
  local copies, waits for them, and re-layouts  6.93 us (3%)
  matrix products  3.95 us (2%)
    pallas_call x1, Pallas kernels, sweeps_on_device(): pl.pallas_call(functools.partial(sweeps_kernel, peers), out_shape=jax.Sha...  124 us
    all_gather x2, waiting for transfers between devices, fetch_velocity(): return lax.all_gather(velocity_x, 'scalar', axis=2, tiled=True)  44.5 us
    pallas_call x2, Pallas kernels, circulant_blocks(): pl.pallas_call(circulant_kernel, grid=(count,), in_specs=[pl.BlockSpec((1...  7.5 us
    unnamed x5, local copies, waits for them, and re-layouts  4.8 us
  transfers between devices with their start and end apart: 2, of which 2 were waited for; matrix products, arithmetic and copies ran while one was open for 3% of the time, Pallas kernels for 4%

profile of v2, /device:TPU:9, one launch (start us, length us, event | category | flops | bytes accessed | tf_op | source)
XLA Modules:
  0.0 202.6 jit_solution(17779766046759863276)
XLA Ops:
  6.5 0.0 copy-start
  6.5 0.0 all-gather.3.cloned.1.call-start
  6.5 0.7 all-gather.3.cloned.1.call-update
  7.3 0.0 all-gather.5.cloned.1.call-start
  7.3 0.7 all-gather.5.cloned.1.call-update
  8.0 0.7 fusion.6
  8.7 0.0 copy-start.1
  8.7 2.8 %fusion = f32[4,1024]{1,0:T(4,128)S(1)} fusion(f32[513,1024]{1,0:T(8,128)} %constant.11.clone, f32[513]{0:T(1024)S(1)} %convert_multiply_fusion, f32[4]{0:T(128)S(1)} %get-tuple-element.14), kind=kOutput, calls=%fused_computation.3 | convolution fusion | flops 25219080 | bytes 2119700 | tf_op jit(solution)/shard_map/dot_general | solution.py:157
  11.5 0.1 slice.10
  11.5 0.1 pad_maximum_fusion
  11.6 0.6 broadcast_in_dim.20.g_ref
  12.3 0.0 copy-done
  12.3 1.2 fusion.1
  13.4 0.6 broadcast_in_dim.21.g_ref
  14.1 0.0 copy-done.1
  14.1 0.8 copy.9.sx_ref
  14.9 3.8 %shard_map.83 = (bf16[4,256,1024]{2,1,0:T(8,128)(2,1)}, bf16[4,256,1024]{2,1,0:T(8,128)(2,1)}) custom-call(f32[4,1,1024]{2,1,0:T(1,128)} %broadcast_in_dim.21.g_ref), custom_call_target="tpu_custom_call" | custom-call | tf_op jit(solution)/shard_map/pallas_call | solution.py:172
  18.6 3.7 %shard_map.82 = (bf16[4,256,1024]{2,1,0:T(8,128)(2,1)}, bf16[4,256,1024]{2,1,0:T(8,128)(2,1)}) custom-call(f32[4,1,1024]{2,1,0:T(1,128)} %broadcast_in_dim.20.g_ref), custom_call_target="tpu_custom_call" | custom-call | tf_op jit(solution)/shard_map/pallas_call | solution.py:172
  22.4 15.4 %all-gather.3.cloned.1.call-done.vx_ref = f32[2,128,1024]{2,1,0:T(8,128)} async-done(((f32[2,128,256]{2,1,0:T(8,128)}), f32[2,128,1024]{2,1,0:T(8,128)}) %all-gather.3.cloned.1.call-update) | async-done | bytes 1048592 | tf_op jit(solution)/shard_map/all_gather | solution.py:103
  37.8 29.0 %all-gather.5.cloned.1.call-done.vy_ref = f32[2,128,1024]{2,1,0:T(8,128)} async-done(((f32[2,128,256]{2,1,0:T(8,128)}), f32[2,128,1024]{2,1,0:T(8,128)}) %all-gather.5.cloned.1.call-update) | async-done | bytes 1048592 | tf_op jit(solution)/shard_map/all_gather | solution.py:103
  66.8 124.1 %shard_map.84 = f32[4,2,128,1024]{3,2,1,0:T(8,128)} custom-call(f32[4,2,128,1024]{3,2,1,0:T(8,128)} %q_ref.1, f32[2,128,1024]{2,1,0:T(8,128)} %all-gather.3.cloned.1.call-done.vx_ref, f32[2,128,1024]{2,1,0:T(8,128)} %all-gather.5.cloned.1.call-done.vy_ref, s32[2,128,1]{2,1,0:T(8,128)} %copy.9.sx_ref, s32[1,128]{1,0:T(1,128)} %bitcast.5, ...), custom_call_target="tpu_custom_call" | custom-call | tf_op jit(solution)/shard_map/pallas_call | solution.py:381
  190.9 4.8 %copy.11 = f32[4,2,128,1024]{3,2,1,0:T(8,128)} copy(f32[4,2,128,1024]{3,2,1,0:T(8,128)} %shard_map.84) | data formatting | bytes 8388608
  (2 shorter events, 0.0 us)
Async XLA Ops:
  6.5 5.7 %copy-start = (f32[513,1024]{1,0:T(8,128)S(1)}, f32[513,1024]{1,0:T(8,128)}, u32[]{:S(2)}) copy-start(f32[513,1024]{1,0:T(8,128)} %constant.11.clone) | copy-start | bytes 6303748
  6.5 31.3 %all-gather.3.cloned.1.call-start = ((), (), s32[]{:S(2)}) async-start(), calls=%async_computation | async-start | bytes 1310720 | tf_op jit(solution)/shard_map/all_gather | solution.py:103
  7.3 59.6 %all-gather.5.cloned.1.call-start = ((), (), s32[]{:S(2)}) async-start(), calls=%async_computation.1 | async-start | bytes 1310720 | tf_op jit(solution)/shard_map/all_gather | solution.py:103
  8.7 5.4 %copy-start.1 = (s32[2,128]{1,0:T(2,128)S(1)}, s32[2,128]{1,0:T(2,128)}, u32[]{:S(2)}) copy-start(s32[2,128]{1,0:T(2,128)} %param.11) | copy-start | bytes 3076
Sparse Core Ops, SparseCore 0:
  8.9 28.8 all-gather.2
  39.4 27.4 all-gather.4

commit v3 on v2

--- a/solution.py
+++ b/solution.py
@@ -188,12 +188,12 @@
 
 
 def sweeps_kernel(
-    peers,
+    peers, groups,
     q_ref, vx_ref, vy_ref, sx_ref, sy_ref, xh_ref, xl_ref, yh_ref, yl_ref,
     out_ref,
     wx, wy, part_hi, part_lo, swept, col_hi, col_lo, tall,
-    ext, cols, turned, back,
-    send1, recv1, send2, recv2,
+    ext, cols, turned, back, held,
+    sendv, recvv, send1, recv1, send2, recv2,
 ):
     ns, nz, rows, nx = q_ref.shape
     ny = rows * peers
@@ -204,16 +204,39 @@
     barrier = pltpu.get_barrier_semaphore()
     for k in range(1, peers):
         pl.semaphore_signal(barrier, inc=1, device_id={"space": lax.rem(me + k, peers)}, device_id_type=MESH)
+    mine = lax.axis_index("scalar")
+    for k in range(1, groups):
+        pl.semaphore_signal(barrier, inc=1, device_id={"scalar": lax.rem(mine + k, groups)}, device_id_type=MESH)
+    pl.semaphore_wait(barrier, peers + groups - 2)
+
+    def spread(n, k):
+        return pltpu.make_async_remote_copy(
+            src_ref=(vx_ref, vy_ref)[n], dst_ref=held.at[n, mine],
+            send_sem=sendv.at[n, k - 1], recv_sem=recvv.at[n, k - 1],
+            device_id={"scalar": lax.rem(mine + k, groups)}, device_id_type=MESH,
+        )
+
+    for n in range(2):
+        for k in range(1, groups):
+            spread(n, k).start()
+    held[0, mine] = vx_ref[...]
+    held[1, mine] = vy_ref[...]
 
     step = 16
     per = rows // step
 
-    @pl.loop(0, nz * per)
-    def _(i):
-        z, r = i // per, pl.multiple_of((i % per) * step, step)
-        for v_ref, w_ref in ((vx_ref, wx), (vy_ref, wy)):
-            for m, w in enumerate(spline_weights(v_ref[z, pl.ds(r, step), :])):
+    def weigh(n, w_ref):
+        for k in range(1, groups):
+            spread(n, k).wait_recv()
+
+        @pl.loop(0, nz * per)
+        def _(i):
+            z, r = i // per, pl.multiple_of((i % per) * step, step)
+            f = jnp.concatenate([held[n, g, z, pl.ds(r, step), :] for g in range(groups)], axis=1)
+            for m, w in enumerate(spline_weights(f)):
                 w_ref[z, m, pl.ds(r, step), :] = w
+
+    weigh(0, wx)
 
     def remesh_rows(load):
         @pl.loop(0, nz * per, unroll=2)
@@ -260,13 +283,15 @@
 
     edge = lax.broadcasted_iota(jnp.int32, (8, width), 0)
 
-    def first(s):
+    def first(s, start):
         remesh_rows(lambda z, r: q_ref[s, z, pl.ds(r, step), :])
 
         def store(c, total):
             swept[:, c:c + BLOCK] = total
 
         diffuse_rows(s, store)
+        if start:
+            weigh(1, wy)
 
         @pl.loop(0, nz * peers)
         def _(i):
@@ -285,15 +310,14 @@
 
     @pl.loop(0, 1)
     def _(s):
-        first(s)
-
-    pl.semaphore_wait(barrier, peers - 1)
+        first(s, True)
+
     for k in range(1, peers):
         forward(0, k).start()
 
     @pl.loop(1, ns)
     def _(s):
-        first(s)
+        first(s, False)
         for k in range(1, peers):
             forward(s, k).start()
 
@@ -364,12 +388,14 @@
             forward(s, k).wait_send()
             backward(s, k).wait_send()
 
-
-def sweeps_on_device(peers, scalars, velocity_x, velocity_y, shift_x, shift_y, schmidt):
+    for n in range(2):
+        for k in range(1, groups):
+            spread(n, k).wait_send()
+
+
+def sweeps_on_device(peers, groups, scalars, velocity_x, velocity_y, shift_x, shift_y, schmidt):
     ns, nz, rows, nx = scalars.shape
     ny, width = rows * peers, nx // peers
-    along_x = fetch_velocity(velocity_x)
-    along_y = fetch_velocity(velocity_y)
     diffusivity = jnp.exp2((3 - schmidt).astype(jnp.float32))
     line_x = jnp.roll(response(0.5 * diffusivity, nx), -(REACH + 2), axis=1)
     line_y = response(diffusivity, ny)
@@ -379,7 +405,7 @@
     vmem = pl.BlockSpec(memory_space=pltpu.VMEM)
     dma = pltpu.SemaphoreType.DMA((ns, peers - 1))
     return pl.pallas_call(
-        functools.partial(sweeps_kernel, peers),
+        functools.partial(sweeps_kernel, peers, groups),
         out_shape=jax.ShapeDtypeStruct(scalars.shape, f32),
         in_specs=[vmem] * 9,
         out_specs=vmem,
@@ -396,13 +422,16 @@
             pltpu.VMEM((ns, peers, nz, rows + 8, width), f32),
             pltpu.VMEM((ns, peers, nz, rows, width), f32),
             pltpu.VMEM((ns, peers, nz, rows, width), f32),
+            pltpu.VMEM((2, groups) + velocity_x.shape, f32),
+            pltpu.SemaphoreType.DMA((2, groups - 1)),
+            pltpu.SemaphoreType.DMA((2, groups - 1)),
             dma, dma, dma, dma,
         ],
         compiler_params=pltpu.CompilerParams(
             collective_id=0, has_side_effects=True, vmem_limit_bytes=62 * 2**20
         ),
     )(
-        scalars, along_x, along_y, shift_x[:, :, None], shift_y[None, :], xh, xl, yh, yl
+        scalars, velocity_x, velocity_y, shift_x[:, :, None], shift_y[None, :], xh, xl, yh, yl
     )
 
 
@@ -412,7 +441,7 @@
 
 def solution(mesh):
     peers = mesh.shape["space"]
-    body = functools.partial(sweeps_on_device, peers) if fits_kernel(mesh) else on_device
+    body = functools.partial(sweeps_on_device, peers, mesh.shape["scalar"]) if fits_kernel(mesh) else on_device
     return jax.shard_map(
         body,
         mesh=mesh,

time: 204 us -> 183 us (0.90)
  waiting for transfers between devices: 45.9 us -> 0 us
  Pallas kernels: 132 us -> 171 us
  between operations: 13.4 us -> 0.02 us
    all_gather x2 -> x0, waiting for transfers between devices: 44.5 us -> none  [fetch_velocity(): return lax.all_gather(velocity_x, 'scalar', axis=2, tiled=True)]
    pallas_call x1, Pallas kernels: 124 us -> 163 us  [sweeps_on_device(): pl.pallas_call(functools.partial(sweeps_kernel, peers, groups), out_shape...]
  transfers between devices with their start and end apart: 2 -> 0, of which waited for: 2 -> 0; matrix products, arithmetic and copies ran while one was open for 3% -> 0% of each run, Pallas kernels for 4% -> 0%
where the time goes in v3:
time: 183 us; the launch traced here: 182 us
  Pallas kernels  171 us (93%)
  local copies, waits for them, and re-layouts  6.91 us (4%)
  matrix products  3.95 us (2%)
    pallas_call x1, Pallas kernels, sweeps_on_device(): pl.pallas_call(functools.partial(sweeps_kernel, peers, groups), out_shape...  163 us
    pallas_call x2, Pallas kernels, circulant_blocks(): pl.pallas_call(circulant_kernel, grid=(count,), in_specs=[pl.BlockSpec((1...  7.56 us
    unnamed x5, local copies, waits for them, and re-layouts  4.8 us
    dot_general x2, matrix products, response(): jnp.dot(damping, table, precision=lax.Precision.HIGHEST, preferred_elemen...  3.95 us

profile of v3, /device:TPU:9, one launch (start us, length us, event | category | flops | bytes accessed | tf_op | source)
XLA Modules:
  0.0 182.5 jit_solution(1054001675302102557)
XLA Ops:
  0.0 0.0 copy-start
  0.0 0.8 fusion.6
  0.8 0.0 copy-start.1
  0.8 2.8 %fusion = f32[4,1024]{1,0:T(4,128)S(1)} fusion(f32[513,1024]{1,0:T(8,128)} %constant.11.clone, f32[513]{0:T(1024)S(1)} %convert_multiply_fusion, f32[4]{0:T(128)S(1)} %get-tuple-element.14), kind=kOutput, calls=%fused_computation.3 | convolution fusion | flops 25219080 | bytes 2119700 | tf_op jit(solution)/shard_map/dot_general | solution.py:157
  3.6 0.1 slice.10
  3.7 0.1 pad_maximum_fusion
  3.8 0.6 broadcast_in_dim.20.g_ref
  4.4 0.0 copy-done
  4.4 1.2 fusion.1
  5.6 0.6 broadcast_in_dim.21.g_ref
  6.2 0.0 copy-done.1
  6.2 0.8 copy.9.sx_ref
  7.0 3.8 %shard_map.83 = (bf16[4,256,1024]{2,1,0:T(8,128)(2,1)}, bf16[4,256,1024]{2,1,0:T(8,128)(2,1)}) custom-call(f32[4,1,1024]{2,1,0:T(1,128)} %broadcast_in_dim.21.g_ref), custom_call_target="tpu_custom_call" | custom-call | tf_op jit(solution)/shard_map/pallas_call | solution.py:172
  10.8 3.7 %shard_map.82 = (bf16[4,256,1024]{2,1,0:T(8,128)(2,1)}, bf16[4,256,1024]{2,1,0:T(8,128)(2,1)}) custom-call(f32[4,1,1024]{2,1,0:T(1,128)} %broadcast_in_dim.20.g_ref), custom_call_target="tpu_custom_call" | custom-call | tf_op jit(solution)/shard_map/pallas_call | solution.py:172
  14.5 163.2 %shard_map.84 = f32[4,2,128,1024]{3,2,1,0:T(8,128)} custom-call(f32[4,2,128,1024]{3,2,1,0:T(8,128)} %q_ref.1, f32[2,128,256]{2,1,0:T(8,128)} %vx_ref.1, f32[2,128,256]{2,1,0:T(8,128)} %vy_ref.1, s32[2,128,1]{2,1,0:T(8,128)} %copy.9.sx_ref, s32[1,128]{1,0:T(1,128)} %bitcast.5, bf16[4,256,1024]{2,1,0:T(8,128)(2,1)} %get-tuple-element.9.xh_ref, ...), custom_call_target="tpu_custom_call" | custom-call | tf_op jit(solution)/shard_map/pallas_call | solution.py:407
  177.7 4.8 %copy.11 = f32[4,2,128,1024]{3,2,1,0:T(8,128)} copy(f32[4,2,128,1024]{3,2,1,0:T(8,128)} %shard_map.84) | data formatting | bytes 8388608
  (2 shorter events, 0.0 us)
Async XLA Ops:
  0.0 4.4 %copy-start = (f32[513,1024]{1,0:T(8,128)S(1)}, f32[513,1024]{1,0:T(8,128)}, u32[]{:S(2)}) copy-start(f32[513,1024]{1,0:T(8,128)} %constant.11.clone) | copy-start | bytes 6303748
  0.8 5.4 %copy-start.1 = (s32[2,128]{1,0:T(2,128)S(1)}, s32[2,128]{1,0:T(2,128)}, u32[]{:S(2)}) copy-start(s32[2,128]{1,0:T(2,128)} %param.11) | copy-start | bytes 3076
